TPU v7x, 32 devices: a whole 2x2x4 slice. The times are simulated.
32 devices in a mesh: seq: 8 (over y, x, core), head: 4 (over z).
Axes of the slice: x: 2, y: 2, z: 4, core: 2. Of those that a mesh axis runs over, the one named last changes fastest.
Arguments:
- queries: bfloat16 [1024, 32, 576], P('seq', 'head'), may hold values from -64 to 64
- latent: bfloat16 [1024, 576], P('seq'), may hold values from -8 to 8
- grad_out: bfloat16 [1024, 32, 512], P('seq', 'head'), may hold values from -6 to 6
- lookback: int32 [1024], P('seq'), may hold values from 0 to 256
Outputs:
- grad_queries: bfloat16 [1024, 32, 576], P('seq', 'head')
- grad_latent: bfloat16 [1024, 576], P('seq')
All inputs are finite; a program needn't handle non-finite values.
Results may differ from a plain program's by a relative error of at most 0.0049.
Values may be sent and summed in bfloat16 or wider, within the bound.
A program may use at most 64 MiB of HBM per device.

v0:
```python
import jax
import jax.numpy as jnp
from jax import lax
from jax.sharding import PartitionSpec as P

ROPE = 64
NOPE = 128


def passed_along(value, axis, steps):
    count = lax.axis_size(axis)
    leading, last = (max(0, -steps), min(count, count - steps))
    return lax.ppermute(value, axis, [(source, source + steps) for source in range(leading, last)])


def attend(query_rows, grad_rows, key_rows, allowed):
    score_scale = (NOPE + ROPE) ** (-0.5)
    value_width = grad_rows.shape[1]
    scores = jnp.dot(query_rows, key_rows.T, preferred_element_type=jnp.float32) * score_scale
    masked = jnp.where(allowed, scores, -jnp.inf)
    highest = jnp.max(masked, axis=-1, keepdims=True)
    weights = jnp.exp(masked - highest)
    weights = weights / jnp.sum(weights, axis=-1, keepdims=True)
    grad_weights = jnp.dot(
        grad_rows, key_rows[:, :value_width].T, preferred_element_type=jnp.float32
    )
    row_dot = jnp.sum(weights * grad_weights, axis=-1, keepdims=True)
    grad_scores = (weights * (grad_weights - row_dot) * score_scale).astype(jnp.bfloat16)
    weights_half = weights.astype(jnp.bfloat16)
    grad_query = jnp.dot(grad_scores, key_rows, preferred_element_type=jnp.float32).astype(
        jnp.bfloat16
    )
    grad_keys = jnp.dot(grad_scores.T, query_rows, preferred_element_type=jnp.float32)
    grad_values = jnp.dot(weights_half.T, grad_rows, preferred_element_type=jnp.float32)
    extra_width = key_rows.shape[1] - value_width
    combined = grad_keys + jnp.pad(grad_values, ((0, 0), (0, extra_width)))
    return (grad_query, combined)


def on_device(queries, latent, grad_out, lookback):
    tok_rows, head_count, key_width = queries.shape
    value_width = grad_out.shape[2]
    earlier = [latent]
    for distance in range(2):
        earlier.append(passed_along(earlier[-1], "seq", 1))
    key_rows = jnp.concatenate([earlier[2], earlier[1], latent], axis=0)
    first_row = lax.axis_index("seq") * tok_rows
    query_pos = first_row + jnp.arange(tok_rows, dtype=jnp.int32)
    key_pos = first_row - 2 * tok_rows + jnp.arange(3 * tok_rows, dtype=jnp.int32)
    allowed = (
        (key_pos[None, :] >= 0)
        & (key_pos[None, :] <= query_pos[:, None])
        & (key_pos[None, :] >= query_pos[:, None] - lookback[:, None])
    )
    allowed = jnp.broadcast_to(allowed[:, None, :], (tok_rows, head_count, 3 * tok_rows)).reshape(
        tok_rows * head_count, 3 * tok_rows
    )
    grad_query, combined = attend(
        queries.reshape(tok_rows * head_count, key_width),
        grad_out.reshape(tok_rows * head_count, value_width),
        key_rows,
        allowed,
    )
    pieces = (combined[:tok_rows], combined[tok_rows : 2 * tok_rows], combined[2 * tok_rows :])
    carried = pieces[0]
    for partial_value in pieces[1:]:
        carried = passed_along(carried, "seq", -1) + partial_value
    summed = lax.psum(carried, "head").astype(jnp.bfloat16)
    return (grad_query.reshape(tok_rows, head_count, key_width), summed)


def solution(mesh):
    return jax.shard_map(
        on_device,
        mesh=mesh,
        in_specs=(P("seq", "head", None), P("seq", None), P("seq", "head", None), P("seq")),
        out_specs=(P("seq", "head", None), P("seq", None)),
        check_vma=False,
    )
```

profile of v0, /device:TPU:4, one launch (start us, length us, event | category | flops | bytes accessed | tf_op | source)
XLA Modules:
  0.0 66.3 jit_solution(2651284842522481367)
XLA Ops:
  0.6 0.0 copy-start
  0.6 0.0 copy-start.2
  0.7 2.1 %collective-permute-start = (bf16[128,576]{0,1:T(8,128)(2,1)}, bf16[128,576]{0,1:T(8,128)(2,1)}, u32[]{:S(2)}, u32[]{:S(2)}) collective-permute-start(bf16[128,576]{0,1:T(8,128)(2,1)} %param.5), channel_id=1, source_target_pairs={{0,4},{4,8},{8,12},{12,16},{16,20},{20,24},{24,28},{1,5},{5,9},{9,... | collective-permute-start | bytes 442376 | tf_op jit(solution)/shard_map/ppermute | solution.py:13
  2.8 0.7 %iota_add_fusion.1 = (s32[128]{0:T(128)S(1)}, s32[128]{0:T(128)S(1)}) fusion(s32[]{:T(128)S(6)} %mul.18, s32[128]{0:T(128)} %param.7), kind=kLoop, calls=%fused_computation.29 | loop fusion | flops 256 | bytes 1540 | tf_op jit(solution)/shard_map/add | solution.py:48
  3.4 0.1 compare_and_fusion
  3.5 4.9 %collective-permute-done = bf16[128,576]{0,1:T(8,128)(2,1)} collective-permute-done((bf16[128,576]{0,1:T(8,128)(2,1)}, bf16[128,576]{0,1:T(8,128)(2,1)}, u32[]{:S(2)}, u32[]{:S(2)}) %collective-permute-start) | collective-permute-done | bytes 147488 | tf_op jit(solution)/shard_map/ppermute | solution.py:13
  8.5 1.9 %collective-permute-start.1 = (bf16[128,576]{0,1:T(8,128)(2,1)}, bf16[128,576]{0,1:T(8,128)(2,1)}, u32[]{:S(2)}, u32[]{:S(2)}) collective-permute-start(bf16[128,576]{0,1:T(8,128)(2,1)} %collective-permute-done), channel_id=1, source_target_pairs={{0,4},{4,8},{8,12},{12,16},{16,20},{20,24},{24,28},{1,5},{5,9},{9,... | collective-permute-start | bytes 442376 | tf_op jit(solution)/shard_map/ppermute | solution.py:13
  10.4 0.2 broadcast_bitcast_fusion
  10.6 1.2 %copy.9 = pred[1024,384]{0,1:T(32,128)(4,1)} copy(pred[1024,384]{1,0:T(32,128)(4,1)S(1)} %broadcast_bitcast_fusion) | data formatting | bytes 786432 | tf_op jit(solution)/shard_map/reshape | solution.py:55
  11.8 0.0 copy-done.2
  11.8 1.3 %copy.8 = bf16[128,8,576]{2,1,0:T(8,128)(2,1)S(1)} copy(bf16[128,8,576]{0,2,1:T(8,128)(2,1)S(1)} %copy-done.2) | data formatting | bytes 2359296 | tf_op args[0]
  13.2 3.0 %collective-permute-done.1 = bf16[128,576]{0,1:T(8,128)(2,1)} collective-permute-done((bf16[128,576]{0,1:T(8,128)(2,1)}, bf16[128,576]{0,1:T(8,128)(2,1)}, u32[]{:S(2)}, u32[]{:S(2)}) %collective-permute-start.1) | collective-permute-done | bytes 147488 | tf_op jit(solution)/shard_map/ppermute | solution.py:13
  16.1 0.9 %constant_dynamic-update-slice_fusion.2 = bf16[384,576]{0,1:T(8,128)(2,1)S(1)} fusion(bf16[128,576]{0,1:T(8,128)(2,1)} %collective-permute-done.1), kind=kLoop, calls=%fused_computation.26 | loop fusion | bytes 294912
  17.1 0.9 %constant_dynamic-update-slice_fusion.1 = bf16[384,576]{0,1:T(8,128)(2,1)S(1)} fusion(bf16[384,576]{0,1:T(8,128)(2,1)S(1)} %constant_dynamic-update-slice_fusion.2, bf16[128,576]{0,1:T(8,128)(2,1)} %collective-permute-done), kind=kLoop, calls=%fused_computation.25 | loop fusion | bytes 294912
  18.0 0.9 %constant_dynamic-update-slice_fusion = bf16[384,576]{0,1:T(8,128)(2,1)S(1)} fusion(bf16[384,576]{0,1:T(8,128)(2,1)S(1)} %constant_dynamic-update-slice_fusion.1, bf16[128,576]{0,1:T(8,128)(2,1)} %param.5), kind=kLoop, calls=%fused_computation.24 | loop fusion | bytes 294912 | tf_op jit(solution)/shard_map/concatenate | solution.py:46
  19.0 1.9 %fusion.16 = (f32[1024]{0:T(1024)S(1)}, f32[1024,384]{0,1:T(8,128)S(1)}) fusion(pred[1024,384]{0,1:T(32,128)(4,1)} %copy.9, bf16[384,576]{0,1:T(8,128)(2,1)S(1)} %constant_dynamic-update-slice_fusion, bf16[128,8,576]{2,1,0:T(8,128)(2,1)S(1)} %copy.8), kind=kOutput, calls=%fused_computation.31 | convolution fusion | flops 454163456 | bytes 3592192 | tf_op jit(solution)/shard_map/dot_general | solution.py:19
  20.9 0.2 fusion.5
  21.1 0.0 copy-done
  21.1 0.7 fusion
  21.8 0.8 %fusion.8 = f32[384,512]{0,1:T(8,128)S(1)} fusion(bf16[128,8,512]{2,1,0:T(8,128)(2,1)S(1)} %copy-done, f32[1024,384]{0,1:T(8,128)S(1)} %get-tuple-element.7, f32[1024]{0:T(1024)S(1)} %fusion.5, f32[1024]{0:T(1024)S(1)} %get-tuple-element.6), kind=kOutput, calls=%fused_computation.14 | convolution fusion | flops 403832832 | bytes 3416064 | tf_op jit(solution)/shard_map/dot_general | solution.py:34
  22.6 0.4 fusion.3
  23.0 0.8 %convolution_add_fusion = f32[384,576]{0,1:T(8,128)S(1)} fusion(bf16[1024,384]{0,1:T(8,128)(2,1)S(1)} %fusion.3, bf16[128,8,576]{2,1,0:T(8,128)(2,1)S(1)} %copy.8, f32[384,512]{0,1:T(8,128)S(1)} %fusion.8), kind=kOutput, calls=%fused_computation.11 | convolution fusion | flops 453206016 | bytes 3637248 | tf_op jit(solution)/shard_map/dot_general | solution.py:33
  23.9 0.0 copy-start.1
  23.9 1.9 %collective-permute-start.2 = (f32[128,576]{0,1:T(8,128)S(1)}, f32[128,576]{0,1:T(8,128)S(1)}, u32[]{:S(2)}, u32[]{:S(2)}) collective-permute-start(f32[128,576]{0,1:T(8,128)S(1)} %slice.17), channel_id=1, source_target_pairs={{4,0},{8,4},{12,8},{16,12},{20,16},{24,20},{28,24},{5,1},{9,5},{13... | collective-permute-start | bytes 884744 | tf_op jit(solution)/shard_map/ppermute | solution.py:13
  25.8 4.2 %collective-permute-done.2 = f32[128,576]{0,1:T(8,128)S(1)} collective-permute-done((f32[128,576]{0,1:T(8,128)S(1)}, f32[128,576]{0,1:T(8,128)S(1)}, u32[]{:S(2)}, u32[]{:S(2)}) %collective-permute-start.2) | collective-permute-done | bytes 294944 | tf_op jit(solution)/shard_map/ppermute | solution.py:13
  30.0 0.7 %slice_add_fusion.1 = f32[128,576]{0,1:T(8,128)} fusion(f32[128,576]{0,1:T(8,128)S(1)} %collective-permute-done.2, f32[384,576]{0,1:T(8,128)S(1)} %convolution_add_fusion), kind=kLoop, calls=%fused_computation.22 | loop fusion | flops 73728 | bytes 884736 | tf_op jit(solution)/shard_map/add | solution.py:67
  30.8 4.7 %collective-permute-start.3 = (f32[128,576]{0,1:T(8,128)}, f32[128,576]{0,1:T(8,128)}, u32[]{:S(2)}, u32[]{:S(2)}) collective-permute-start(f32[128,576]{0,1:T(8,128)} %slice_add_fusion.1), channel_id=1, source_target_pairs={{4,0},{8,4},{12,8},{16,12},{20,16},{24,20},{28,24},{5,1},{9,5},{13... | collective-permute-start | bytes 884744 | tf_op jit(solution)/shard_map/ppermute | solution.py:13
  35.5 0.0 copy-done.1
  35.5 0.8 %convolution_convert_fusion = bf16[1024,576]{0,1:T(8,128)(2,1)S(1)} fusion(bf16[384,576]{0,1:T(8,128)(2,1)S(1)} %constant_dynamic-update-slice_fusion, bf16[1024,384]{0,1:T(8,128)(2,1)S(1)} %fusion.3), kind=kOutput, calls=%fused_computation.8 | convolution fusion | flops 453574656 | bytes 2408448 | tf_op jit(solution)/shard_map/dot_general | solution.py:30
  36.3 0.7 %copy.10 = bf16[1024,576]{1,0:T(8,128)(2,1)S(1)} copy(bf16[1024,576]{0,1:T(8,128)(2,1)S(1)} %convolution_convert_fusion) | data formatting | bytes 2359296 | tf_op jit(solution)/shard_map/convert_element_type | solution.py:30
  37.0 1.8 %copy.12 = bf16[128,8,576]{0,2,1:T(8,128)(2,1)} copy(bf16[128,8,576]{2,1,0:T(8,128)(2,1)S(1)} %bitcast.34) | data formatting | bytes 2359296
  38.8 1.2 %collective-permute-done.3 = f32[128,576]{0,1:T(8,128)} collective-permute-done((f32[128,576]{0,1:T(8,128)}, f32[128,576]{0,1:T(8,128)}, u32[]{:S(2)}, u32[]{:S(2)}) %collective-permute-start.3) | collective-permute-done | bytes 294944 | tf_op jit(solution)/shard_map/ppermute | solution.py:13
  40.0 1.1 %slice_add_fusion = f32[128,576]{0,1:T(8,128)S(1)} fusion(f32[128,576]{0,1:T(8,128)} %collective-permute-done.3, f32[384,576]{0,1:T(8,128)} %copy-done.1), kind=kLoop, calls=%fused_computation.21 | loop fusion | flops 73728 | bytes 884736 | tf_op jit(solution)/shard_map/add | solution.py:67
  41.1 25.2 %all-reduce.2 = bf16[128,576]{0,1:T(8,128)(2,1)} all-reduce(f32[128,576]{0,1:T(8,128)S(1)} %slice_add_fusion), channel_id=1, replica_groups=mesh['seq'=8,'head'=4] {'head'}, use_global_device_ids=true, to_apply=%region_3.4 | all-reduce | flops 73728 | bytes 442368 | tf_op jit(solution)/shard_map/psum | solution.py:68
  (3 shorter events, 0.0 us)
Async XLA Ops:
  0.6 20.5 %copy-start = (bf16[128,8,512]{2,1,0:T(8,128)(2,1)S(1)}, bf16[128,8,512]{2,1,0:T(8,128)(2,1)}, u32[]{:S(2)}) copy-start(bf16[128,8,512]{2,1,0:T(8,128)(2,1)} %param.6) | copy-start | bytes 3145732
  0.6 11.2 %copy-start.2 = (bf16[128,8,576]{0,2,1:T(8,128)(2,1)S(1)}, bf16[128,8,576]{0,2,1:T(8,128)(2,1)}, u32[]{:S(2)}) copy-start(bf16[128,8,576]{0,2,1:T(8,128)(2,1)} %param.4) | copy-start | bytes 3538948
  0.7 7.8 %collective-permute-start = (bf16[128,576]{0,1:T(8,128)(2,1)}, bf16[128,576]{0,1:T(8,128)(2,1)}, u32[]{:S(2)}, u32[]{:S(2)}) collective-permute-start(bf16[128,576]{0,1:T(8,128)(2,1)} %param.5), channel_id=1, source_target_pairs={{0,4},{4,8},{8,12},{12,16},{16,20},{20,24},{24,28},{1,5},{5,9},{9,... | collective-permute-start | bytes 442376 | tf_op jit(solution)/shard_map/ppermute | solution.py:13
  8.5 7.7 %collective-permute-start.1 = (bf16[128,576]{0,1:T(8,128)(2,1)}, bf16[128,576]{0,1:T(8,128)(2,1)}, u32[]{:S(2)}, u32[]{:S(2)}) collective-permute-start(bf16[128,576]{0,1:T(8,128)(2,1)} %collective-permute-done), channel_id=1, source_target_pairs={{0,4},{4,8},{8,12},{12,16},{16,20},{20,24},{24,28},{1,5},{5,9},{9,... | collective-permute-start | bytes 442376 | tf_op jit(solution)/shard_map/ppermute | solution.py:13
  23.9 11.6 %copy-start.1 = (f32[384,576]{0,1:T(8,128)}, f32[384,576]{0,1:T(8,128)S(1)}, u32[]{:S(2)}) copy-start(f32[384,576]{0,1:T(8,128)S(1)} %convolution_add_fusion) | copy-start | bytes 2654212
  23.9 6.1 %collective-permute-start.2 = (f32[128,576]{0,1:T(8,128)S(1)}, f32[128,576]{0,1:T(8,128)S(1)}, u32[]{:S(2)}, u32[]{:S(2)}) collective-permute-start(f32[128,576]{0,1:T(8,128)S(1)} %slice.17), channel_id=1, source_target_pairs={{4,0},{8,4},{12,8},{16,12},{20,16},{24,20},{28,24},{5,1},{9,5},{13... | collective-permute-start | bytes 884744 | tf_op jit(solution)/shard_map/ppermute | solution.py:13
  30.8 9.2 %collective-permute-start.3 = (f32[128,576]{0,1:T(8,128)}, f32[128,576]{0,1:T(8,128)}, u32[]{:S(2)}, u32[]{:S(2)}) collective-permute-start(f32[128,576]{0,1:T(8,128)} %slice_add_fusion.1), channel_id=1, source_target_pairs={{4,0},{8,4},{12,8},{16,12},{20,16},{24,20},{28,24},{5,1},{9,5},{13... | collective-permute-start | bytes 884744 | tf_op jit(solution)/shard_map/ppermute | solution.py:13
where the time goes:
time: 66.6 us; the launch traced here: 66.3 us
  blocking collectives  25.2 us (38%)
  waiting for transfers between devices  13.4 us (20%)
  starting transfers between devices  10.6 us (16%)
  local copies, waits for them, and re-layouts  8.12 us (12%)
  matrix products  4.96 us (7%)
  other arithmetic  3.29 us (5%)
  between operations  0.81 us (1%)
    psum x1, blocking collectives, on_device(): summed = lax.psum(carried, 'head').astype(jnp.bfloat16)  25.2 us
    ppermute x4, waiting for transfers between devices, passed_along(): lax.ppermute(value, axis, [(source, source + steps) for source in range(l...  13.4 us
    ppermute x4, starting transfers between devices, passed_along(): lax.ppermute(value, axis, [(source, source + steps) for source in range(l...  10.6 us
    unnamed x10, local copies, waits for them, and re-layouts  5.02 us
    dot_general x1, matrix products, attend(): jnp.dot(query_rows, key_rows.T, preferred_element_type=jnp.float32)  1.91 us
    add x2, other arithmetic, on_device(): carried = passed_along(carried, 'seq', -1) + partial_value  1.83 us
    reshape x2, local copies, waits for them, and re-layouts, on_device(): jnp.broadcast_to(allowed[:, None, :], (tok_rows, head_count, 3 * tok_rows))  1.41 us
  transfers between devices with their start and end apart: 4, of which 4 were waited for; matrix products, arithmetic and copies ran while one was open for 10% of the time, Pallas kernels for 0%

commit v1 on v0

v1 whole, which is shorter than its diff:
```python
import functools

import jax
import jax.numpy as jnp
from jax import lax
from jax.experimental import pallas as pl
from jax.experimental.pallas import tpu as pltpu
from jax.sharding import PartitionSpec as P

ROPE = 64
NOPE = 128
MESH = pl.DeviceIdType.MESH
F32 = jnp.float32
BF16 = jnp.bfloat16


def dot(a, b, trans_b=False):
    dims = (((1,), (1 if trans_b else 0,)), ((), ()))
    return lax.dot_general(a, b, dims, preferred_element_type=F32)


def kernel(
    n_seq, n_head, rows,
    q_hbm, k_hbm, g_hbm, look_ref, gq_hbm, gl_ref,
    q_v, g_v, g_wide, g_t, keys_t, keys, scores, grad_w, d_scores, weights, gq_v,
    part_out, part_in, own_sum, head_out, head_in, final,
    load_sem, gq_sem, key_send, key_recv, part_send, part_recv,
    head_send, head_recv, final_send, final_recv,
):
    heads, key_width, tok = q_hbm.shape
    value_width = g_hbm.shape[1]
    cols = heads * tok
    scale = (NOPE + ROPE) ** (-0.5)
    seq, head = lax.axis_index("seq"), lax.axis_index("head")
    ahead = [lax.rem(seq + d, n_seq) for d in (1, 2)]
    behind = [lax.rem(seq + n_seq - d, n_seq) for d in (1, 2)]
    peers = [lax.rem(head + 1 + i, n_head) for i in range(n_head - 1)]

    own_copy = pltpu.make_async_copy(k_hbm, keys_t.at[2], load_sem.at[0])
    own_copy.start()
    g_copy = pltpu.make_async_copy(g_hbm, g_v, load_sem.at[1])
    g_copy.start()
    q_copies = [
        pltpu.make_async_copy(q_hbm.at[h], q_v.at[:, h * tok:(h + 1) * tok], load_sem.at[2 + h])
        for h in range(heads)
    ]
    for copy in q_copies:
        copy.start()

    barrier = pltpu.get_barrier_semaphore()
    for other in ahead + behind:
        pl.semaphore_signal(barrier, inc=1, device_id=(other, head), device_id_type=MESH)
    for other in peers:
        pl.semaphore_signal(barrier, inc=1, device_id=(seq, other), device_id_type=MESH)
    pl.semaphore_wait(barrier, 4 + n_head - 1)

    own_copy.wait()
    key_copies = [
        pltpu.make_async_remote_copy(
            src_ref=keys_t.at[2], dst_ref=keys_t.at[1 - d],
            send_sem=key_send.at[d], recv_sem=key_recv.at[d],
            device_id=(ahead[d], head), device_id_type=MESH,
        )
        for d in range(2)
    ]
    for copy in key_copies:
        copy.start()

    keys[2 * tok:, :] = keys_t[2].T
    g_copy.wait()
    for c in range(value_width // 128):
        part = slice(c * 128, (c + 1) * 128)
        g_wide[c] = g_v[:, part].astype(F32)
        for h in range(heads):
            block = g_wide[c, pl.ds(h, tok, stride=heads), :].astype(BF16)
            g_t[part, h * tok:(h + 1) * tok] = block.T
    for copy in q_copies:
        copy.wait()
    own_keys = keys[2 * tok:, :]
    scores[2 * tok:, :] = dot(own_keys, q_v[...])
    grad_w[2 * tok:, :] = dot(own_keys[:, :value_width], g_t[...])

    for copy in key_copies:
        copy.wait_recv()
    for d in range(2):
        keys[d * tok:(d + 1) * tok, :] = keys_t[d].T
    far_keys = keys[:2 * tok, :]
    scores[:2 * tok, :] = dot(far_keys, q_v[...])
    grad_w[:2 * tok, :] = dot(far_keys[:, :value_width], g_t[...])

    key_pos = lax.broadcasted_iota(jnp.int32, (3 * tok, tok), 0)
    query_pos = lax.broadcasted_iota(jnp.int32, (3 * tok, tok), 1) + 2 * tok
    allowed = (
        (key_pos <= query_pos)
        & (key_pos >= query_pos - look_ref[...])
        & (key_pos >= (2 - seq) * tok)
    )
    for h in range(heads):
        span = slice(h * tok, (h + 1) * tok)
        masked = jnp.where(allowed, scores[:, span] * scale, -jnp.inf)
        weight = jnp.exp(masked - jnp.max(masked, axis=0, keepdims=True))
        weight = weight * (1.0 / jnp.sum(weight, axis=0, keepdims=True))
        grad_weight = grad_w[:, span]
        row_dot = jnp.sum(weight * grad_weight, axis=0, keepdims=True)
        d_scores[:, span] = (weight * (grad_weight - row_dot) * scale).astype(BF16)
        weights[:, span] = weight.astype(BF16)

    def partial_sum(first, last):
        q_part = dot(q_v[...], d_scores[first:last, :], True)
        g_part = dot(g_t[...], weights[first:last, :], True)
        return q_part[:value_width] + g_part, q_part[value_width:]

    top, bottom = partial_sum(0, 2 * tok)
    for d in range(2):
        part_out[d, :value_width, :] = top[:, d * tok:(d + 1) * tok].astype(BF16)
        part_out[d, value_width:key_width, :] = bottom[:, d * tok:(d + 1) * tok].astype(BF16)

    def piece(i):
        return pl.ds(pl.multiple_of(lax.rem(head + 1 + i, n_head) * rows, 16), rows)

    part_copies = []
    for i in range(n_head):
        for d in range(2):
            copy = pltpu.make_async_remote_copy(
                src_ref=part_out.at[d, piece(i)], dst_ref=part_in.at[d, piece(i)],
                send_sem=part_send.at[d, i], recv_sem=part_recv.at[d, i],
                device_id=(behind[1 - d], head), device_id_type=MESH,
            )
            copy.start()
            part_copies.append(copy)

    top, bottom = partial_sum(2 * tok, 3 * tok)
    own_sum[:value_width, :] = top
    own_sum[value_width:key_width, :] = bottom

    def reduce_piece(i):
        for copy in part_copies[2 * i:2 * i + 2]:
            copy.wait_recv()
        here = piece(i)
        return own_sum[here, :] + part_in[0, here, :].astype(F32) + part_in[1, here, :].astype(F32)

    gq_copies = []

    def grad_queries(first, last):
        all_keys = jnp.concatenate([keys_t[0], keys_t[1], keys_t[2]], axis=1)
        span = slice(first * tok, last * tok)
        gq_v[:, span] = dot(all_keys, d_scores[:, span]).astype(BF16)
        for h in range(first, last):
            copy = pltpu.make_async_copy(
                gq_v.at[:, h * tok:(h + 1) * tok], gq_hbm.at[h], gq_sem.at[h]
            )
            copy.start()
            gq_copies.append(copy)

    grad_queries(0, heads)

    head_copies = []
    for i in range(n_head - 1):
        head_out[i] = reduce_piece(i).astype(BF16)
        copy = pltpu.make_async_remote_copy(
            src_ref=head_out.at[i], dst_ref=head_in.at[i],
            send_sem=head_send.at[i], recv_sem=head_recv.at[i],
            device_id=(seq, peers[i]), device_id_type=MESH,
        )
        copy.start()
        head_copies.append(copy)
    total = reduce_piece(n_head - 1)
    for i in range(n_head - 1):
        head_copies[i].wait_recv()
        total = total + head_in[i].astype(F32)
    mine = piece(n_head - 1)
    final[mine, :] = total.astype(BF16)
    final_copies = []
    for i in range(n_head - 1):
        copy = pltpu.make_async_remote_copy(
            src_ref=final.at[mine], dst_ref=final.at[mine],
            send_sem=final_send.at[i], recv_sem=final_recv.at[i],
            device_id=(seq, peers[i]), device_id_type=MESH,
        )
        copy.start()
        final_copies.append(copy)
    for copy in final_copies:
        copy.wait_recv()
    gl_ref[...] = final[:key_width, :]
    for copy in key_copies + part_copies + head_copies + final_copies:
        copy.wait_send()
    for copy in gq_copies:
        copy.wait()


def on_device(n_seq, n_head, queries, latent, grad_out, lookback):
    tok, heads, key_width = queries.shape
    value_width = grad_out.shape[2]
    cols = heads * tok
    rows = -(-key_width // (n_head * 16)) * 16
    padded = rows * n_head
    dma = pltpu.SemaphoreType.DMA
    flops = 2 * 3 * tok * cols * (3 * key_width + 2 * value_width)
    grad_q, grad_l = pl.pallas_call(
        functools.partial(kernel, n_seq, n_head, rows),
        out_shape=(
            jax.ShapeDtypeStruct((heads, key_width, tok), BF16),
            jax.ShapeDtypeStruct((key_width, tok), BF16),
        ),
        in_specs=[pl.BlockSpec(memory_space=pl.ANY)] * 3
        + [pl.BlockSpec(memory_space=pltpu.VMEM)],
        out_specs=(pl.BlockSpec(memory_space=pl.ANY), pl.BlockSpec(memory_space=pltpu.VMEM)),
        scratch_shapes=[
            pltpu.VMEM((key_width, cols), BF16),
            pltpu.VMEM((cols, value_width), BF16),
            pltpu.VMEM((value_width // 128, cols, 128), F32),
            pltpu.VMEM((value_width, cols), BF16),
            pltpu.VMEM((3, key_width, tok), BF16),
            pltpu.VMEM((3 * tok, key_width), BF16),
            pltpu.VMEM((3 * tok, cols), F32),
            pltpu.VMEM((3 * tok, cols), F32),
            pltpu.VMEM((3 * tok, cols), BF16),
            pltpu.VMEM((3 * tok, cols), BF16),
            pltpu.VMEM((key_width, cols), BF16),
            pltpu.VMEM((2, padded, tok), BF16),
            pltpu.VMEM((2, padded, tok), BF16),
            pltpu.VMEM((padded, tok), F32),
            pltpu.VMEM((n_head - 1, rows, tok), BF16),
            pltpu.VMEM((n_head - 1, rows, tok), BF16),
            pltpu.VMEM((padded, tok), BF16),
            dma((2 + heads,)),
            dma((heads,)),
            dma((2,)),
            dma((2,)),
            dma((2, n_head)),
            dma((2, n_head)),
            dma((n_head - 1,)),
            dma((n_head - 1,)),
            dma((n_head - 1,)),
            dma((n_head - 1,)),
        ],
        compiler_params=pltpu.CompilerParams(
            collective_id=0, has_side_effects=True, vmem_limit_bytes=40 * 1024 * 1024
        ),
        cost_estimate=pl.CostEstimate(
            flops=flops, bytes_accessed=8 * cols * key_width, transcendentals=3 * tok * cols
        ),
        name="latent_backward",
    )(
        queries.transpose(1, 2, 0),
        latent.T,
        grad_out.reshape(tok * heads, value_width),
        lookback.reshape(1, tok),
    )
    return grad_q.transpose(2, 0, 1), grad_l.T


def solution(mesh):
    return jax.shard_map(
        functools.partial(on_device, mesh.shape["seq"], mesh.shape["head"]),
        mesh=mesh,
        in_specs=(P("seq", "head", None), P("seq", None), P("seq", "head", None), P("seq")),
        out_specs=(P("seq", "head", None), P("seq", None)),
        check_vma=False,
    )
```

time: 66.6 us -> 35.6 us (0.53)
  the two profiles are of different devices: /device:TPU:4 before, /device:TPU:0 now
where the time goes in v1:
time: 35.6 us; the launch traced here: 35.3 us
  Pallas kernels  29 us (81%)
  local copies, waits for them, and re-layouts  5.73 us (16%)
  between operations  0.65 us (2%)
    pallas_call x1, Pallas kernels, on_device(): pl.pallas_call(functools.partial(kernel, n_seq, n_head, rows), out_shape=...  29 us
    unnamed x10, local copies, waits for them, and re-layouts  5.73 us

profile of v1, /device:TPU:0, one launch (start us, length us, event | category | flops | bytes accessed | tf_op | source)
XLA Modules:
  0.0 35.3 jit_solution(2253233236174330454)
XLA Ops:
  0.6 0.0 copy-start
  0.6 1.3 %copy-done = bf16[128,8,576]{0,2,1:T(8,128)(2,1)S(1)} copy-done((bf16[128,8,576]{0,2,1:T(8,128)(2,1)S(1)}, bf16[128,8,576]{0,2,1:T(8,128)(2,1)}, u32[]{:S(2)}) %copy-start) | copy-done | bytes 1179672
  1.9 0.0 copy-start.1
  1.9 1.2 %copy-done.1 = bf16[128,8,512]{2,1,0:T(8,128)(2,1)S(1)} copy-done((bf16[128,8,512]{2,1,0:T(8,128)(2,1)S(1)}, bf16[128,8,512]{2,1,0:T(8,128)(2,1)}, u32[]{:S(2)}) %copy-start.1) | copy-done | bytes 1048600
  3.1 0.0 copy-start.2
  3.1 0.9 %copy-done.2 = bf16[128,576]{0,1:T(8,128)(2,1)S(1)} copy-done((bf16[128,576]{0,1:T(8,128)(2,1)S(1)}, bf16[128,576]{0,1:T(8,128)(2,1)}, u32[]{:S(2)}) %copy-start.2) | copy-done | bytes 147480
  4.0 0.0 copy-start.3
  4.0 0.7 %copy-done.3 = s32[128]{0:T(128)S(1)} copy-done((s32[128]{0:T(128)S(1)}, s32[128]{0:T(128)}, u32[]{:S(2)}) %copy-start.3) | copy-done | bytes 536
  4.7 29.0 %latent_backward.1 = (bf16[8,576,128]{2,1,0:T(8,128)(2,1)S(1)}, bf16[576,128]{1,0:T(8,128)(2,1)S(1)}) custom-call(bf16[8,576,128]{2,1,0:T(8,128)(2,1)S(1)} %bitcast.8, bf16[576,128]{1,0:T(8,128)(2,1)S(1)} %bitcast.10, bf16[1024,512]{1,0:T(8,128)(2,1)S(1)} %bitcast.9, s32[1,128]{1,0:T(1,128)S(1)} %bitcast.11), custom_call_target="tpu_custom_call" | custom-call | flops 2164260864 | bytes 4718592 | tf_op jit(solution)/shard_map/latent_backward/pallas_call | solution.py:199
  33.7 1.0 %copy.8 = bf16[128,8,576]{0,2,1:T(8,128)(2,1)} copy(bf16[128,8,576]{0,2,1:T(8,128)(2,1)S(1)} %bitcast.6) | data formatting | bytes 2359296
  34.7 0.7 %copy.9 = bf16[128,576]{0,1:T(8,128)(2,1)} copy(bf16[128,576]{0,1:T(8,128)(2,1)S(1)} %bitcast.7) | data formatting | bytes 294912
Async XLA Ops:
  0.6 1.3 %copy-start = (bf16[128,8,576]{0,2,1:T(8,128)(2,1)S(1)}, bf16[128,8,576]{0,2,1:T(8,128)(2,1)}, u32[]{:S(2)}) copy-start(bf16[128,8,576]{0,2,1:T(8,128)(2,1)} %param.4) | copy-start | bytes 3538948
  1.9 1.2 %copy-start.1 = (bf16[128,8,512]{2,1,0:T(8,128)(2,1)S(1)}, bf16[128,8,512]{2,1,0:T(8,128)(2,1)}, u32[]{:S(2)}) copy-start(bf16[128,8,512]{2,1,0:T(8,128)(2,1)} %param.6) | copy-start | bytes 3145732
  3.1 0.9 %copy-start.2 = (bf16[128,576]{0,1:T(8,128)(2,1)S(1)}, bf16[128,576]{0,1:T(8,128)(2,1)}, u32[]{:S(2)}) copy-start(bf16[128,576]{0,1:T(8,128)(2,1)} %param.5) | copy-start | bytes 442372
  4.0 0.7 %copy-start.3 = (s32[128]{0:T(128)S(1)}, s32[128]{0:T(128)}, u32[]{:S(2)}) copy-start(s32[128]{0:T(128)} %param.7) | copy-start | bytes 1540

commit v2 on v1

--- a/solution.py
+++ b/solution.py
@@ -21,8 +21,8 @@
 
 def kernel(
     n_seq, n_head, rows,
-    q_hbm, k_hbm, g_hbm, look_ref, gq_hbm, gl_ref,
-    q_v, g_v, g_wide, g_t, keys_t, keys, scores, grad_w, d_scores, weights, gq_v,
+    q_hbm, k_hbm, g_hbm, look_hbm, gq_hbm, gl_ref,
+    look_ref, q_v, g_v, g_wide, g_t, keys_t, keys, scores, grad_w, d_scores, weights, gq_v,
     part_out, part_in, own_sum, head_out, head_in, final,
     load_sem, gq_sem, key_send, key_recv, part_send, part_recv,
     head_send, head_recv, final_send, final_recv,
@@ -44,7 +44,8 @@
         pltpu.make_async_copy(q_hbm.at[h], q_v.at[:, h * tok:(h + 1) * tok], load_sem.at[2 + h])
         for h in range(heads)
     ]
-    for copy in q_copies:
+    look_copy = pltpu.make_async_copy(look_hbm, look_ref, load_sem.at[2 + heads])
+    for copy in q_copies + [look_copy]:
         copy.start()
 
     barrier = pltpu.get_barrier_semaphore()
@@ -88,6 +89,7 @@
     scores[:2 * tok, :] = dot(far_keys, q_v[...])
     grad_w[:2 * tok, :] = dot(far_keys[:, :value_width], g_t[...])
 
+    look_copy.wait()
     key_pos = lax.broadcasted_iota(jnp.int32, (3 * tok, tok), 0)
     query_pos = lax.broadcasted_iota(jnp.int32, (3 * tok, tok), 1) + 2 * tok
     allowed = (
@@ -188,6 +190,17 @@
         copy.wait()
 
 
+def write_back(gq_ref, gl_ref, gq_out, gl_out, sem):
+    heads = gq_ref.shape[0]
+    copies = [pltpu.make_async_copy(gl_ref, gl_out, sem.at[heads])]
+    for h in range(heads):
+        copies.append(pltpu.make_async_copy(gq_ref.at[h], gq_out.at[h], sem.at[h]))
+    for copy in copies:
+        copy.start()
+    for copy in copies:
+        copy.wait()
+
+
 def on_device(n_seq, n_head, queries, latent, grad_out, lookback):
     tok, heads, key_width = queries.shape
     value_width = grad_out.shape[2]
@@ -196,16 +209,25 @@
     padded = rows * n_head
     dma = pltpu.SemaphoreType.DMA
     flops = 2 * 3 * tok * cols * (3 * key_width + 2 * value_width)
+    operands = [
+        pltpu.with_memory_space_constraint(value, pltpu.HBM)
+        for value in (
+            queries.transpose(1, 2, 0),
+            latent.T,
+            grad_out.reshape(tok * heads, value_width),
+            lookback.reshape(1, tok),
+        )
+    ]
     grad_q, grad_l = pl.pallas_call(
         functools.partial(kernel, n_seq, n_head, rows),
         out_shape=(
             jax.ShapeDtypeStruct((heads, key_width, tok), BF16),
             jax.ShapeDtypeStruct((key_width, tok), BF16),
         ),
-        in_specs=[pl.BlockSpec(memory_space=pl.ANY)] * 3
-        + [pl.BlockSpec(memory_space=pltpu.VMEM)],
+        in_specs=[pl.BlockSpec(memory_space=pltpu.HBM)] * 4,
         out_specs=(pl.BlockSpec(memory_space=pl.ANY), pl.BlockSpec(memory_space=pltpu.VMEM)),
         scratch_shapes=[
+            pltpu.VMEM((1, tok), jnp.int32),
             pltpu.VMEM((key_width, cols), BF16),
             pltpu.VMEM((cols, value_width), BF16),
             pltpu.VMEM((value_width // 128, cols, 128), F32),
@@ -223,7 +245,7 @@
             pltpu.VMEM((n_head - 1, rows, tok), BF16),
             pltpu.VMEM((n_head - 1, rows, tok), BF16),
             pltpu.VMEM((padded, tok), BF16),
-            dma((2 + heads,)),
+            dma((3 + heads,)),
             dma((heads,)),
             dma((2,)),
             dma((2,)),
@@ -241,12 +263,18 @@
             flops=flops, bytes_accessed=8 * cols * key_width, transcendentals=3 * tok * cols
         ),
         name="latent_backward",
-    )(
-        queries.transpose(1, 2, 0),
-        latent.T,
-        grad_out.reshape(tok * heads, value_width),
-        lookback.reshape(1, tok),
-    )
+    )(*operands)
+    grad_q, grad_l = pl.pallas_call(
+        write_back,
+        out_shape=(
+            jax.ShapeDtypeStruct(grad_q.shape, BF16),
+            jax.ShapeDtypeStruct(grad_l.shape, BF16),
+        ),
+        in_specs=[pl.BlockSpec(memory_space=pl.ANY)] * 2,
+        out_specs=(pl.BlockSpec(memory_space=pltpu.HBM),) * 2,
+        scratch_shapes=[dma((heads + 1,))],
+        name="write_back",
+    )(grad_q, grad_l)
     return grad_q.transpose(2, 0, 1), grad_l.T
 
 

time: 35.6 us -> 72.4 us (2.03)
  Pallas kernels: 29 us -> 69.9 us
  local copies, waits for them, and re-layouts: 5.73 us -> 1.66 us
    pallas_call x0 -> x1, Pallas kernels: none -> 41.4 us  [on_device(): pl.pallas_call(write_back, out_shape=(jax.ShapeDtypeStruct(grad_q.shape,...]
    unnamed x10 -> x4, local copies, waits for them, and re-layouts: 5.73 us -> 1.66 us
where the time goes in v2:
time: 72.4 us; the launch traced here: 72.2 us
  Pallas kernels  69.9 us (97%)
  local copies, waits for them, and re-layouts  1.66 us (2%)
    pallas_call x1, Pallas kernels, on_device(): pl.pallas_call(write_back, out_shape=(jax.ShapeDtypeStruct(grad_q.shape,...  41.4 us
    pallas_call x1, Pallas kernels, on_device(): pl.pallas_call(functools.partial(kernel, n_seq, n_head, rows), out_shape=...  28.6 us
    unnamed x4, local copies, waits for them, and re-layouts  1.66 us

profile of v2, /device:TPU:0, one launch (start us, length us, event | category | flops | bytes accessed | tf_op | source)
XLA Modules:
  0.0 72.2 jit_solution(9335181310514335976)
XLA Ops:
  0.6 28.6 %latent_backward.1 = (bf16[8,576,128]{2,1,0:T(8,128)(2,1)S(1)}, bf16[576,128]{1,0:T(8,128)(2,1)S(1)}) custom-call(bf16[8,576,128]{2,1,0:T(8,128)(2,1)} %bitcast.6, bf16[576,128]{1,0:T(8,128)(2,1)} %bitcast.9, bf16[1024,512]{1,0:T(8,128)(2,1)} %bitcast.8, s32[1,128]{1,0:T(1,128)} %bitcast.11), custom_call_target="tpu_custom_call" | custom-call | flops 2164260864 | bytes 4718592 | tf_op jit(solution)/shard_map/latent_backward/pallas_call | solution.py:221
  29.2 0.0 copy-start
  29.2 1.0 %copy-done = bf16[8,576,128]{2,1,0:T(8,128)(2,1)} copy-done((bf16[8,576,128]{2,1,0:T(8,128)(2,1)}, bf16[8,576,128]{2,1,0:T(8,128)(2,1)S(1)}, u32[]{:S(2)}) %copy-start) | copy-done | bytes 1179672
  30.2 0.0 copy-start.1
  30.2 0.6 copy-done.1
  30.9 41.4 %write_back.1 = (bf16[8,576,128]{2,1,0:T(8,128)(2,1)}, bf16[576,128]{1,0:T(8,128)(2,1)}) custom-call(bf16[8,576,128]{2,1,0:T(8,128)(2,1)} %copy-done, bf16[576,128]{1,0:T(8,128)(2,1)} %copy-done.1), custom_call_target="tpu_custom_call" | custom-call | tf_op jit(solution)/shard_map/write_back/pallas_call | solution.py:267
Async XLA Ops:
  29.2 1.0 %copy-start = (bf16[8,576,128]{2,1,0:T(8,128)(2,1)}, bf16[8,576,128]{2,1,0:T(8,128)(2,1)S(1)}, u32[]{:S(2)}) copy-start(bf16[8,576,128]{2,1,0:T(8,128)(2,1)S(1)} %get-tuple-element.6.gq_ref) | copy-start | bytes 3538948
  30.2 0.7 copy-start.1

commit v3 on v2

--- a/solution.py
+++ b/solution.py
@@ -9,6 +9,7 @@
 
 ROPE = 64
 NOPE = 128
+KEY_CHUNKS = 4
 MESH = pl.DeviceIdType.MESH
 F32 = jnp.float32
 BF16 = jnp.bfloat16
@@ -23,8 +24,8 @@
     n_seq, n_head, rows,
     q_hbm, k_hbm, g_hbm, look_hbm, gq_hbm, gl_ref,
     look_ref, q_v, g_v, g_wide, g_t, keys_t, keys, scores, grad_w, d_scores, weights, gq_v,
-    part_out, part_in, own_sum, head_out, head_in, final,
-    load_sem, gq_sem, key_send, key_recv, part_send, part_recv,
+    part_out, part_in, relay_in, own_sum, head_out, head_in, final,
+    load_sem, gq_sem, key_send, key_recv, part_send, part_recv, relay_recv,
     head_send, head_recv, final_send, final_recv,
 ):
     heads, key_width, tok = q_hbm.shape
@@ -56,16 +57,27 @@
     pl.semaphore_wait(barrier, 4 + n_head - 1)
 
     own_copy.wait()
-    key_copies = [
-        pltpu.make_async_remote_copy(
-            src_ref=keys_t.at[2], dst_ref=keys_t.at[1 - d],
-            send_sem=key_send.at[d], recv_sem=key_recv.at[d],
-            device_id=(ahead[d], head), device_id_type=MESH,
-        )
-        for d in range(2)
-    ]
-    for copy in key_copies:
-        copy.start()
+    even = lax.rem(seq, 2) == 0
+    chunk = key_width // KEY_CHUNKS
+
+    def send_keys(source, target, c, other):
+        span = pl.ds(c * chunk, chunk)
+        return pltpu.make_async_remote_copy(
+            src_ref=keys_t.at[source, span], dst_ref=keys_t.at[target, span],
+            send_sem=key_send.at[source, target, c], recv_sem=key_recv.at[target, c],
+            device_id=(other, head), device_id_type=MESH,
+        )
+
+    near_keys = [send_keys(2, 1, c, ahead[0]) for c in range(KEY_CHUNKS)]
+    far_sends = [send_keys(2, 0, c, ahead[1]) for c in range(KEY_CHUNKS)]
+    passed_on = [send_keys(1, 0, c, ahead[0]) for c in range(KEY_CHUNKS)]
+    for copy in near_keys:
+        copy.start()
+
+    @pl.when(even)
+    def _():
+        for copy in far_sends:
+            copy.start()
 
     keys[2 * tok:, :] = keys_t[2].T
     g_copy.wait()
@@ -81,7 +93,18 @@
     scores[2 * tok:, :] = dot(own_keys, q_v[...])
     grad_w[2 * tok:, :] = dot(own_keys[:, :value_width], g_t[...])
 
-    for copy in key_copies:
+    @pl.when(even)
+    def _():
+        for c in range(KEY_CHUNKS):
+            near_keys[c].wait_recv()
+            passed_on[c].start()
+
+    @pl.when(jnp.logical_not(even))
+    def _():
+        for copy in near_keys:
+            copy.wait_recv()
+
+    for copy in far_sends:
         copy.wait_recv()
     for d in range(2):
         keys[d * tok:(d + 1) * tok, :] = keys_t[d].T
@@ -120,24 +143,47 @@
     def piece(i):
         return pl.ds(pl.multiple_of(lax.rem(head + 1 + i, n_head) * rows, 16), rows)
 
-    part_copies = []
-    for i in range(n_head):
-        for d in range(2):
-            copy = pltpu.make_async_remote_copy(
-                src_ref=part_out.at[d, piece(i)], dst_ref=part_in.at[d, piece(i)],
-                send_sem=part_send.at[d, i], recv_sem=part_recv.at[d, i],
-                device_id=(behind[1 - d], head), device_id_type=MESH,
-            )
+    def send_part(source, target_ref, recv_sem, i, other):
+        return pltpu.make_async_remote_copy(
+            src_ref=part_out.at[source, piece(i)], dst_ref=target_ref.at[piece(i)],
+            send_sem=part_send.at[source, i], recv_sem=recv_sem.at[i],
+            device_id=(other, head), device_id_type=MESH,
+        )
+
+    far_parts = [send_part(0, part_in.at[0], part_recv.at[0], i, behind[1]) for i in range(n_head)]
+    near_parts = [send_part(1, part_in.at[1], part_recv.at[1], i, behind[0]) for i in range(n_head)]
+    relayed = [send_part(0, relay_in, relay_recv, i, behind[0]) for i in range(n_head)]
+
+    @pl.when(even)
+    def _():
+        for copy in far_parts:
             copy.start()
-            part_copies.append(copy)
+        for i in range(n_head):
+            here = piece(i)
+            relayed[i].wait_recv()
+            joined = part_out[1, here, :].astype(F32) + relay_in[here, :].astype(F32)
+            part_out[1, here, :] = joined.astype(BF16)
+            near_parts[i].start()
+
+    @pl.when(jnp.logical_not(even))
+    def _():
+        part_in[0] = jnp.zeros_like(part_in[0])
+        for i in range(n_head):
+            relayed[i].start()
+        for copy in near_parts:
+            copy.start()
 
     top, bottom = partial_sum(2 * tok, 3 * tok)
     own_sum[:value_width, :] = top
     own_sum[value_width:key_width, :] = bottom
 
     def reduce_piece(i):
-        for copy in part_copies[2 * i:2 * i + 2]:
-            copy.wait_recv()
+        near_parts[i].wait_recv()
+
+        @pl.when(even)
+        def _():
+            far_parts[i].wait_recv()
+
         here = piece(i)
         return own_sum[here, :] + part_in[0, here, :].astype(F32) + part_in[1, here, :].astype(F32)
 
@@ -184,8 +230,19 @@
     for copy in final_copies:
         copy.wait_recv()
     gl_ref[...] = final[:key_width, :]
-    for copy in key_copies + part_copies + head_copies + final_copies:
+    for copy in near_keys + near_parts + head_copies + final_copies:
         copy.wait_send()
+
+    @pl.when(even)
+    def _():
+        for copy in far_sends + passed_on + far_parts:
+            copy.wait_send()
+
+    @pl.when(jnp.logical_not(even))
+    def _():
+        for copy in relayed:
+            copy.wait_send()
+
     for copy in gq_copies:
         copy.wait()
 
@@ -241,16 +298,18 @@
             pltpu.VMEM((key_width, cols), BF16),
             pltpu.VMEM((2, padded, tok), BF16),
             pltpu.VMEM((2, padded, tok), BF16),
+            pltpu.VMEM((padded, tok), BF16),
             pltpu.VMEM((padded, tok), F32),
             pltpu.VMEM((n_head - 1, rows, tok), BF16),
             pltpu.VMEM((n_head - 1, rows, tok), BF16),
             pltpu.VMEM((padded, tok), BF16),
             dma((3 + heads,)),
             dma((heads,)),
-            dma((2,)),
-            dma((2,)),
+            dma((3, 2, KEY_CHUNKS)),
+            dma((2, KEY_CHUNKS)),
             dma((2, n_head)),
             dma((2, n_head)),
+            dma((n_head,)),
             dma((n_head - 1,)),
             dma((n_head - 1,)),
             dma((n_head - 1,)),
@@ -270,7 +329,7 @@
             jax.ShapeDtypeStruct(grad_q.shape, BF16),
             jax.ShapeDtypeStruct(grad_l.shape, BF16),
         ),
-        in_specs=[pl.BlockSpec(memory_space=pl.ANY)] * 2,
+        in_specs=[pl.BlockSpec(memory_space=pltpu.VMEM)] * 2,
         out_specs=(pl.BlockSpec(memory_space=pltpu.HBM),) * 2,
         scratch_shapes=[dma((heads + 1,))],
         name="write_back",

time: 72.4 us -> 32 us (0.44)
  Pallas kernels: 69.9 us -> 29.5 us
    pallas_call x1, Pallas kernels: 41.4 us -> 2.4 us  [on_device(): pl.pallas_call(write_back, out_shape=(jax.ShapeDtypeStruct(grad_q.shape,...]
    pallas_call x1, Pallas kernels: 28.6 us -> 27.1 us  [on_device(): pl.pallas_call(functools.partial(kernel, n_seq, n_head, rows), out_shape=...]
where the time goes in v3:
time: 32 us; the launch traced here: 31.8 us
  Pallas kernels  29.5 us (92%)
  local copies, waits for them, and re-layouts  1.66 us (5%)
  between operations  0.65 us (2%)
    pallas_call x1, Pallas kernels, on_device(): pl.pallas_call(functools.partial(kernel, n_seq, n_head, rows), out_shape=...  27.1 us
    pallas_call x1, Pallas kernels, on_device(): pl.pallas_call(write_back, out_shape=(jax.ShapeDtypeStruct(grad_q.shape,...  2.4 us
    unnamed x4, local copies, waits for them, and re-layouts  1.66 us

profile of v3, /device:TPU:0, one launch (start us, length us, event | category | flops | bytes accessed | tf_op | source)
XLA Modules:
  0.0 31.8 jit_solution(7379114529103323032)
XLA Ops:
  0.6 27.1 %latent_backward.1 = (bf16[8,576,128]{2,1,0:T(8,128)(2,1)S(1)}, bf16[576,128]{1,0:T(8,128)(2,1)S(1)}) custom-call(bf16[8,576,128]{2,1,0:T(8,128)(2,1)} %bitcast.6, bf16[576,128]{1,0:T(8,128)(2,1)} %bitcast.9, bf16[1024,512]{1,0:T(8,128)(2,1)} %bitcast.8, s32[1,128]{1,0:T(1,128)} %bitcast.11), custom_call_target="tpu_custom_call" | custom-call | flops 2164260864 | bytes 4718592 | tf_op jit(solution)/shard_map/latent_backward/pallas_call | solution.py:278
  27.7 0.0 copy-start
  27.7 1.0 %copy-done = bf16[8,576,128]{2,1,0:T(8,128)(2,1)} copy-done((bf16[8,576,128]{2,1,0:T(8,128)(2,1)}, bf16[8,576,128]{2,1,0:T(8,128)(2,1)S(1)}, u32[]{:S(2)}) %copy-start) | copy-done | bytes 1179672
  28.8 0.0 copy-start.1
  28.8 0.6 %copy-done.1 = bf16[576,128]{1,0:T(8,128)(2,1)} copy-done((bf16[576,128]{1,0:T(8,128)(2,1)}, bf16[576,128]{1,0:T(8,128)(2,1)S(1)}, u32[]{:S(2)}) %copy-start.1) | copy-done | bytes 147480
  29.4 2.4 %write_back.1 = (bf16[8,576,128]{2,1,0:T(8,128)(2,1)}, bf16[576,128]{1,0:T(8,128)(2,1)}) custom-call(bf16[8,576,128]{2,1,0:T(8,128)(2,1)} %copy-done, bf16[576,128]{1,0:T(8,128)(2,1)} %copy-done.1), custom_call_target="tpu_custom_call" | custom-call | tf_op jit(solution)/shard_map/write_back/pallas_call | solution.py:326
Async XLA Ops:
  27.7 1.0 %copy-start = (bf16[8,576,128]{2,1,0:T(8,128)(2,1)}, bf16[8,576,128]{2,1,0:T(8,128)(2,1)S(1)}, u32[]{:S(2)}) copy-start(bf16[8,576,128]{2,1,0:T(8,128)(2,1)S(1)} %get-tuple-element.6.gq_ref) | copy-start | bytes 3538948
  28.8 0.7 %copy-start.1 = (bf16[576,128]{1,0:T(8,128)(2,1)}, bf16[576,128]{1,0:T(8,128)(2,1)S(1)}, u32[]{:S(2)}) copy-start(bf16[576,128]{1,0:T(8,128)(2,1)S(1)} %get-tuple-element.7.gl_ref) | copy-start | bytes 442372

commit v4 on v3

--- a/solution.py
+++ b/solution.py
@@ -10,6 +10,7 @@
 ROPE = 64
 NOPE = 128
 KEY_CHUNKS = 4
+LOG2E = 1.4426950408889634
 MESH = pl.DeviceIdType.MESH
 F32 = jnp.float32
 BF16 = jnp.bfloat16
@@ -23,7 +24,7 @@
 def kernel(
     n_seq, n_head, rows,
     q_hbm, k_hbm, g_hbm, look_hbm, gq_hbm, gl_ref,
-    look_ref, q_v, g_v, g_wide, g_t, keys_t, keys, scores, grad_w, d_scores, weights, gq_v,
+    look_ref, q_v, g_v, g_wide, g_t, keys_t, keys, scores, grad_w, bias, part_sum, d_scores, weights, gq_v,
     part_out, part_in, relay_in, own_sum, head_out, head_in, final,
     load_sem, gq_sem, key_send, key_recv, part_send, part_recv, relay_recv,
     head_send, head_recv, final_send, final_recv,
@@ -32,6 +33,7 @@
     value_width = g_hbm.shape[1]
     cols = heads * tok
     scale = (NOPE + ROPE) ** (-0.5)
+    scale2 = scale * LOG2E
     seq, head = lax.axis_index("seq"), lax.axis_index("head")
     ahead = [lax.rem(seq + d, n_seq) for d in (1, 2)]
     behind = [lax.rem(seq + n_seq - d, n_seq) for d in (1, 2)]
@@ -89,29 +91,6 @@
             g_t[part, h * tok:(h + 1) * tok] = block.T
     for copy in q_copies:
         copy.wait()
-    own_keys = keys[2 * tok:, :]
-    scores[2 * tok:, :] = dot(own_keys, q_v[...])
-    grad_w[2 * tok:, :] = dot(own_keys[:, :value_width], g_t[...])
-
-    @pl.when(even)
-    def _():
-        for c in range(KEY_CHUNKS):
-            near_keys[c].wait_recv()
-            passed_on[c].start()
-
-    @pl.when(jnp.logical_not(even))
-    def _():
-        for copy in near_keys:
-            copy.wait_recv()
-
-    for copy in far_sends:
-        copy.wait_recv()
-    for d in range(2):
-        keys[d * tok:(d + 1) * tok, :] = keys_t[d].T
-    far_keys = keys[:2 * tok, :]
-    scores[:2 * tok, :] = dot(far_keys, q_v[...])
-    grad_w[:2 * tok, :] = dot(far_keys[:, :value_width], g_t[...])
-
     look_copy.wait()
     key_pos = lax.broadcasted_iota(jnp.int32, (3 * tok, tok), 0)
     query_pos = lax.broadcasted_iota(jnp.int32, (3 * tok, tok), 1) + 2 * tok
@@ -120,22 +99,75 @@
         & (key_pos >= query_pos - look_ref[...])
         & (key_pos >= (2 - seq) * tok)
     )
-    for h in range(heads):
+    bias[...] = jnp.where(allowed, 0.0, -jnp.inf)
+    own_keys = keys[2 * tok:, :]
+    for h in range(0, heads, 2):
+        span = slice(h * tok, (h + 2) * tok)
+        own_bias = bias[2 * tok:, :]
+        scores[2 * tok:, span] = dot(own_keys, q_v[:, span]) * scale2 + jnp.concatenate(
+            [own_bias, own_bias], axis=1
+        )
+        grad_w[2 * tok:, span] = dot(own_keys[:, :value_width], g_t[:, span])
+
+    @pl.when(even)
+    def _():
+        for c in range(KEY_CHUNKS):
+            near_keys[c].wait_recv()
+            passed_on[c].start()
+
+    @pl.when(jnp.logical_not(even))
+    def _():
+        for copy in near_keys:
+            copy.wait_recv()
+
+    for copy in far_sends:
+        copy.wait_recv()
+    for d in range(2):
+        keys[d * tok:(d + 1) * tok, :] = keys_t[d].T
+    far_keys = keys[:2 * tok, :]
+
+    def far_scores(h):
+        span = slice(h * tok, (h + 2) * tok)
+        scores[:2 * tok, span] = dot(far_keys, q_v[:, span])
+        grad_w[:2 * tok, span] = dot(far_keys[:, :value_width], g_t[:, span])
+
+    def softmax(h):
         span = slice(h * tok, (h + 1) * tok)
-        masked = jnp.where(allowed, scores[:, span] * scale, -jnp.inf)
-        weight = jnp.exp(masked - jnp.max(masked, axis=0, keepdims=True))
-        weight = weight * (1.0 / jnp.sum(weight, axis=0, keepdims=True))
-        grad_weight = grad_w[:, span]
-        row_dot = jnp.sum(weight * grad_weight, axis=0, keepdims=True)
-        d_scores[:, span] = (weight * (grad_weight - row_dot) * scale).astype(BF16)
-        weights[:, span] = weight.astype(BF16)
-
-    def partial_sum(first, last):
-        q_part = dot(q_v[...], d_scores[first:last, :], True)
-        g_part = dot(g_t[...], weights[first:last, :], True)
+        far = scores[:2 * tok, span] * scale2 + bias[:2 * tok, :]
+        own = scores[2 * tok:, span]
+        highest = jnp.maximum(
+            jnp.max(far, axis=0, keepdims=True), jnp.max(own, axis=0, keepdims=True)
+        )
+        exps = [jnp.exp2(far - highest), jnp.exp2(own - highest)]
+        grads = [grad_w[:2 * tok, span], grad_w[2 * tok:, span]]
+        total = sum(jnp.sum(e, axis=0, keepdims=True) for e in exps)
+        inverse = 1.0 / total
+        row_dot = inverse * sum(
+            jnp.sum(e * g, axis=0, keepdims=True) for e, g in zip(exps, grads)
+        )
+        for e, g, rows_of in zip(exps, grads, (slice(0, 2 * tok), slice(2 * tok, 3 * tok))):
+            weight = e * inverse
+            d_scores[rows_of, span] = (weight * (g - row_dot) * scale).astype(BF16)
+            weights[rows_of, span] = weight.astype(BF16)
+
+    def partial_sum(first, last, span):
+        q_part = dot(q_v[:, span], d_scores[first:last, span], True)
+        g_part = dot(g_t[:, span], weights[first:last, span], True)
         return q_part[:value_width] + g_part, q_part[value_width:]
 
-    top, bottom = partial_sum(0, 2 * tok)
+    far_scores(0)
+    for h in range(0, heads, 2):
+        if h + 2 < heads:
+            far_scores(h + 2)
+        softmax(h)
+        softmax(h + 1)
+        top, bottom = partial_sum(0, 2 * tok, slice(h * tok, (h + 2) * tok))
+        if h > 0:
+            top = top + part_sum[:value_width, :]
+            bottom = bottom + part_sum[value_width:, :]
+        if h + 2 < heads:
+            part_sum[:value_width, :] = top
+            part_sum[value_width:, :] = bottom
     for d in range(2):
         part_out[d, :value_width, :] = top[:, d * tok:(d + 1) * tok].astype(BF16)
         part_out[d, value_width:key_width, :] = bottom[:, d * tok:(d + 1) * tok].astype(BF16)
@@ -173,7 +205,7 @@
         for copy in near_parts:
             copy.start()
 
-    top, bottom = partial_sum(2 * tok, 3 * tok)
+    top, bottom = partial_sum(2 * tok, 3 * tok, slice(0, cols))
     own_sum[:value_width, :] = top
     own_sum[value_width:key_width, :] = bottom
 
@@ -293,6 +325,8 @@
             pltpu.VMEM((3 * tok, key_width), BF16),
             pltpu.VMEM((3 * tok, cols), F32),
             pltpu.VMEM((3 * tok, cols), F32),
+            pltpu.VMEM((3 * tok, tok), F32),
+            pltpu.VMEM((key_width, 2 * tok), F32),
             pltpu.VMEM((3 * tok, cols), BF16),
             pltpu.VMEM((3 * tok, cols), BF16),
             pltpu.VMEM((key_width, cols), BF16),
@@ -329,9 +363,10 @@
             jax.ShapeDtypeStruct(grad_q.shape, BF16),
             jax.ShapeDtypeStruct(grad_l.shape, BF16),
         ),
-        in_specs=[pl.BlockSpec(memory_space=pltpu.VMEM)] * 2,
+        in_specs=[pl.BlockSpec(memory_space=pl.ANY)] * 2,
         out_specs=(pl.BlockSpec(memory_space=pltpu.HBM),) * 2,
         scratch_shapes=[dma((heads + 1,))],
+        compiler_params=pltpu.CompilerParams(vmem_limit_bytes=1024 * 1024),
         name="write_back",
     )(grad_q, grad_l)
     return grad_q.transpose(2, 0, 1), grad_l.T

time: 32 us -> 28.2 us (0.88)
  Pallas kernels: 29.5 us -> 27.5 us
  local copies, waits for them, and re-layouts: 1.66 us -> 0 us
    unnamed x4 -> x0, local copies, waits for them, and re-layouts: 1.66 us -> none
    pallas_call x1, Pallas kernels: 2.4 us -> 1.13 us  [on_device(): pl.pallas_call(write_back, out_shape=(jax.ShapeDtypeStruct(grad_q.shape,...]
    pallas_call x1, Pallas kernels: 27.1 us -> 26.3 us  [on_device(): pl.pallas_call(functools.partial(kernel, n_seq, n_head, rows), out_shape=...]
where the time goes in v4:
time: 28.2 us; the launch traced here: 28.1 us
  Pallas kernels  27.5 us (98%)
  between operations  0.64 us (2%)
    pallas_call x1, Pallas kernels, on_device(): pl.pallas_call(functools.partial(kernel, n_seq, n_head, rows), out_shape=...  26.3 us
    pallas_call x1, Pallas kernels, on_device(): pl.pallas_call(write_back, out_shape=(jax.ShapeDtypeStruct(grad_q.shape,...  1.13 us

profile of v4, /device:TPU:0, one launch (start us, length us, event | category | flops | bytes accessed | tf_op | source)
XLA Modules:
  0.0 28.1 jit_solution(7351933608237420105)
XLA Ops:
  0.6 26.3 %latent_backward.1 = (bf16[8,576,128]{2,1,0:T(8,128)(2,1)S(1)}, bf16[576,128]{1,0:T(8,128)(2,1)S(1)}) custom-call(bf16[8,576,128]{2,1,0:T(8,128)(2,1)} %bitcast.6, bf16[576,128]{1,0:T(8,128)(2,1)} %bitcast.9, bf16[1024,512]{1,0:T(8,128)(2,1)} %bitcast.8, s32[1,128]{1,0:T(1,128)} %bitcast.11), custom_call_target="tpu_custom_call" | custom-call | flops 2164260864 | bytes 4718592 | tf_op jit(solution)/shard_map/latent_backward/pallas_call | solution.py:310
  27.0 1.1 %write_back.1 = (bf16[8,576,128]{2,1,0:T(8,128)(2,1)}, bf16[576,128]{1,0:T(8,128)(2,1)}) custom-call(bf16[8,576,128]{2,1,0:T(8,128)(2,1)S(1)} %get-tuple-element.6.gq_ref, bf16[576,128]{1,0:T(8,128)(2,1)S(1)} %get-tuple-element.7.gl_ref), custom_call_target="tpu_custom_call" | custom-call | tf_op jit(solution)/shard_map/write_back/pallas_call | solution.py:360

commit v5 on v4

--- a/solution.py
+++ b/solution.py
@@ -190,24 +190,27 @@
     def _():
         for copy in far_parts:
             copy.start()
+
+    @pl.when(jnp.logical_not(even))
+    def _():
+        part_in[0] = jnp.zeros_like(part_in[0])
+        for i in range(n_head):
+            relayed[i].start()
+        for copy in near_parts:
+            copy.start()
+
+    top, bottom = partial_sum(2 * tok, 3 * tok, slice(0, cols))
+    own_sum[:value_width, :] = top
+    own_sum[value_width:key_width, :] = bottom
+
+    @pl.when(even)
+    def _():
         for i in range(n_head):
             here = piece(i)
             relayed[i].wait_recv()
             joined = part_out[1, here, :].astype(F32) + relay_in[here, :].astype(F32)
             part_out[1, here, :] = joined.astype(BF16)
             near_parts[i].start()
-
-    @pl.when(jnp.logical_not(even))
-    def _():
-        part_in[0] = jnp.zeros_like(part_in[0])
-        for i in range(n_head):
-            relayed[i].start()
-        for copy in near_parts:
-            copy.start()
-
-    top, bottom = partial_sum(2 * tok, 3 * tok, slice(0, cols))
-    own_sum[:value_width, :] = top
-    own_sum[value_width:key_width, :] = bottom
 
     def reduce_piece(i):
         near_parts[i].wait_recv()
@@ -232,8 +235,6 @@
             copy.start()
             gq_copies.append(copy)
 
-    grad_queries(0, heads)
-
     head_copies = []
     for i in range(n_head - 1):
         head_out[i] = reduce_piece(i).astype(BF16)
@@ -244,6 +245,8 @@
         )
         copy.start()
         head_copies.append(copy)
+    grad_queries(0, heads)
+
     total = reduce_piece(n_head - 1)
     for i in range(n_head - 1):
         head_copies[i].wait_recv()

time: 28.2 us -> 27.8 us (0.986)
  Pallas kernels: 27.5 us -> 27 us
    pallas_call x1, Pallas kernels: 26.3 us -> 25.9 us  [on_device(): pl.pallas_call(functools.partial(kernel, n_seq, n_head, rows), out_shape=...]
where the time goes in v5:
time: 27.8 us; the launch traced here: 27.7 us
  Pallas kernels  27 us (97%)
  between operations  0.64 us (2%)
    pallas_call x1, Pallas kernels, on_device(): pl.pallas_call(functools.partial(kernel, n_seq, n_head, rows), out_shape=...  25.9 us
    pallas_call x1, Pallas kernels, on_device(): pl.pallas_call(write_back, out_shape=(jax.ShapeDtypeStruct(grad_q.shape,...  1.13 us

profile of v5, /device:TPU:0, one launch (start us, length us, event | category | flops | bytes accessed | tf_op | source)
XLA Modules:
  0.0 27.7 jit_solution(4213054661169233486)
XLA Ops:
  0.6 25.9 %latent_backward.1 = (bf16[8,576,128]{2,1,0:T(8,128)(2,1)S(1)}, bf16[576,128]{1,0:T(8,128)(2,1)S(1)}) custom-call(bf16[8,576,128]{2,1,0:T(8,128)(2,1)} %bitcast.6, bf16[576,128]{1,0:T(8,128)(2,1)} %bitcast.9, bf16[1024,512]{1,0:T(8,128)(2,1)} %bitcast.8, s32[1,128]{1,0:T(1,128)} %bitcast.11), custom_call_target="tpu_custom_call" | custom-call | flops 2164260864 | bytes 4718592 | tf_op jit(solution)/shard_map/latent_backward/pallas_call | solution.py:313
  26.5 1.1 %write_back.1 = (bf16[8,576,128]{2,1,0:T(8,128)(2,1)}, bf16[576,128]{1,0:T(8,128)(2,1)}) custom-call(bf16[8,576,128]{2,1,0:T(8,128)(2,1)S(1)} %get-tuple-element.6.gq_ref, bf16[576,128]{1,0:T(8,128)(2,1)S(1)} %get-tuple-element.7.gl_ref), custom_call_target="tpu_custom_call" | custom-call | tf_op jit(solution)/shard_map/write_back/pallas_call | solution.py:363

commit v6 on v5

--- a/solution.py
+++ b/solution.py
@@ -52,14 +52,29 @@
         copy.start()
 
     barrier = pltpu.get_barrier_semaphore()
-    for other in ahead + behind:
-        pl.semaphore_signal(barrier, inc=1, device_id=(other, head), device_id_type=MESH)
+    even = lax.rem(seq, 2) == 0
+
+    def greet(other_seq, other_head):
+        pl.semaphore_signal(
+            barrier, inc=1, device_id=(other_seq, other_head), device_id_type=MESH
+        )
+
+    for other in (ahead[0], behind[0]):
+        greet(other, head)
     for other in peers:
-        pl.semaphore_signal(barrier, inc=1, device_id=(seq, other), device_id_type=MESH)
-    pl.semaphore_wait(barrier, 4 + n_head - 1)
+        greet(seq, other)
+
+    @pl.when(even)
+    def _():
+        for other in (ahead[1], behind[1]):
+            greet(other, head)
+        pl.semaphore_wait(barrier, 4 + n_head - 1)
+
+    @pl.when(jnp.logical_not(even))
+    def _():
+        pl.semaphore_wait(barrier, 2 + n_head - 1)
 
     own_copy.wait()
-    even = lax.rem(seq, 2) == 0
     chunk = key_width // KEY_CHUNKS
 
     def send_keys(source, target, c, other):

time: 27.8 us -> 27.2 us (0.978)
  Pallas kernels: 27 us -> 26.4 us
    pallas_call x1, Pallas kernels: 25.9 us -> 25.3 us  [on_device(): pl.pallas_call(functools.partial(kernel, n_seq, n_head, rows), out_shape=...]
where the time goes in v6:
time: 27.2 us; the launch traced here: 27 us
  Pallas kernels  26.4 us (97%)
  between operations  0.64 us (2%)
    pallas_call x1, Pallas kernels, on_device(): pl.pallas_call(functools.partial(kernel, n_seq, n_head, rows), out_shape=...  25.3 us
    pallas_call x1, Pallas kernels, on_device(): pl.pallas_call(write_back, out_shape=(jax.ShapeDtypeStruct(grad_q.shape,...  1.13 us

profile of v6, /device:TPU:0, one launch (start us, length us, event | category | flops | bytes accessed | tf_op | source)
XLA Modules:
  0.0 27.0 jit_solution(2916381639181921270)
XLA Ops:
  0.6 25.3 %latent_backward.1 = (bf16[8,576,128]{2,1,0:T(8,128)(2,1)S(1)}, bf16[576,128]{1,0:T(8,128)(2,1)S(1)}) custom-call(bf16[8,576,128]{2,1,0:T(8,128)(2,1)} %bitcast.6, bf16[576,128]{1,0:T(8,128)(2,1)} %bitcast.9, bf16[1024,512]{1,0:T(8,128)(2,1)} %bitcast.8, s32[1,128]{1,0:T(1,128)} %bitcast.11), custom_call_target="tpu_custom_call" | custom-call | flops 2164260864 | bytes 4718592 | tf_op jit(solution)/shard_map/latent_backward/pallas_call | solution.py:328
  25.9 1.1 %write_back.1 = (bf16[8,576,128]{2,1,0:T(8,128)(2,1)}, bf16[576,128]{1,0:T(8,128)(2,1)}) custom-call(bf16[8,576,128]{2,1,0:T(8,128)(2,1)S(1)} %get-tuple-element.6.gq_ref, bf16[576,128]{1,0:T(8,128)(2,1)S(1)} %get-tuple-element.7.gl_ref), custom_call_target="tpu_custom_call" | custom-call | tf_op jit(solution)/shard_map/write_back/pallas_call | solution.py:378
